TPU v7x, 512 devices: a whole 4x8x8 slice. The times are simulated.
512 devices in a mesh: head: 8 (over y), blk: 64 (over z, x, core).
Axes of the slice: x: 4, y: 8, z: 8, core: 2. Of those that a mesh axis runs over, the one named last changes fastest.
Arguments:
- residual: bfloat16 [12288, 2048], P('blk'), may hold values from -100 to 100
- lengths: int32 [64, 6], P('blk'), may hold values from 1 to 96, 192 in all within a row
- token_adapter_index: int32 [12288, 1], P('blk'), may hold values from 0 to 63; in each aligned block of 192 rows (0 to 191, 192 to 383, ...) at most 6 rows name the same one
- attention_norm_gain: float32 [2048], replicated, may hold values from 0.1 to 1.9
- query_key_weight: bfloat16 [2048, 4096], P('blk', 'head'), may hold values from -8 to 8
- value_weight: bfloat16 [2048, 2048], P('blk', 'head'), may hold values from -0.125 to 0.125
- head_second_weight: float32 [8], P('head'), may hold values from 0.2 to 0.8
- output_weight: bfloat16 [2048, 2048], P('blk', 'head'), may hold values from -0.125 to 0.125
- adapter_down_maps: bfloat16 [64, 2048, 16], P('blk', 'head'), may hold values from -0.125 to 0.125
- adapter_up_maps: bfloat16 [64, 16, 2048], P('blk'), may hold values from -1.5 to 1.5
- feedforward_norm_gain: float32 [2048], replicated, may hold values from 0.1 to 1.9
- gate_weight: bfloat16 [2048, 5632], P('blk', 'head'), may hold values from -0.125 to 0.125
- up_weight: bfloat16 [2048, 5632], P('blk', 'head'), may hold values from -0.125 to 0.125
- down_weight: bfloat16 [2048, 5632], P('blk', 'head'), may hold values from -0.078125 to 0.078125
Outputs:
- layer_out: bfloat16 [12288, 2048], P('blk', 'head')
Inputs may be any that keep to these rules, and one draw needn't show every extreme that they name: `lengths`: each row sums to 192, and its largest entry is 96. `token_adapter_index`: among the 192 tokens of one block no adapter is named more than 6 times, a bound that some block reaches.
All inputs are finite; a program needn't handle non-finite values.
Results may differ from a plain program's by a relative error of at most 0.011.
Values may be sent and summed in bfloat16 or wider, within the bound.
No kernel may reach another device: no remote copies, remote signals or barrier semaphores. Data moves between devices by JAX's collectives and lax.ppermute only.
A program may use at most 64 MiB of HBM per device.

v0:
```python
import jax
import jax.numpy as jnp
from jax import lax
from jax.sharding import PartitionSpec as P

HD = 128
adapter_scaling = 2.0
head_shrink = 0.8
neg_large = -1e30


def rms_scale(values, epsilon):
    return values * lax.rsqrt(jnp.mean(values * values, axis=-1, keepdims=True) + epsilon)


def masked_softmax(scores, allowed):
    scores = jnp.where(allowed, scores, neg_large)
    row_peak = jnp.max(scores, axis=-1, keepdims=True)
    raised = jnp.where(allowed, jnp.exp(scores - row_peak), 0.0)
    return raised / jnp.sum(raised, axis=-1, keepdims=True)


def request_mask(lengths_row, length_total):
    ends_at = jnp.cumsum(lengths_row)
    position = jnp.arange(length_total, dtype=jnp.int32)
    request = jnp.sum((position[:, None] >= ends_at[None, :]).astype(jnp.int32), axis=1)
    return (request[:, None] == request[None, :]) & (position[None, :] <= position[:, None])


def diff_head(qk_head, value_head, allowed, lambda_value):
    score_scale = 1.0 / qk_head.shape[-1] ** 0.5
    first_scores = (
        jnp.dot(qk_head[:, 0], qk_head[:, 2].T, precision=lax.Precision.HIGHEST) * score_scale
    )
    second_scores = (
        jnp.dot(qk_head[:, 1], qk_head[:, 3].T, precision=lax.Precision.HIGHEST) * score_scale
    )
    mixed = (
        masked_softmax(first_scores, allowed)
        - lambda_value * masked_softmax(second_scores, allowed)
    ).astype(jnp.bfloat16)
    attended = jnp.dot(mixed, value_head, preferred_element_type=jnp.float32)
    return (rms_scale(attended, 1e-05) * head_shrink).astype(jnp.bfloat16)


def weight_fold(leading, trailing, combine, initial):
    return combine(
        initial,
        (
            lax.all_gather(leading, "blk", axis=0, tiled=True),
            lax.all_gather(trailing, "blk", axis=0, tiled=True),
        ),
        jnp.int32(0),
    )


def head_total(partial_value):
    return lax.psum_scatter(
        partial_value.astype(jnp.bfloat16), "head", scatter_dimension=1, tiled=True
    ).astype(jnp.float32)


def row_products(source):

    def add_rows(totals, pieces, offset):
        return (
            jnp.dot(source, pieces[0], preferred_element_type=jnp.float32),
            jnp.dot(source, pieces[1], preferred_element_type=jnp.float32),
        )

    return add_rows


def per_device(
    residual,
    lengths,
    token_adapter_index,
    attention_norm_gain,
    query_key_weight,
    value_weight,
    head_second_weight,
    output_weight,
    adapter_down_maps,
    adapter_up_maps,
    feedforward_norm_gain,
    gate_weight,
    up_weight,
    down_weight,
):
    tokens = residual.shape[0]
    width = residual.shape[1]
    owners = lax.axis_size("blk")
    capacity = 2 * tokens // owners
    own_width = width // lax.axis_size("head")
    own_begin = lax.axis_index("head") * own_width
    inputs = residual.astype(jnp.float32)
    normed = (rms_scale(inputs, 1e-06) * attention_norm_gain).astype(jnp.bfloat16)
    qk_start = jnp.zeros((tokens, query_key_weight.shape[1]), jnp.float32)
    value_start = jnp.zeros((tokens, value_weight.shape[1]), jnp.float32)
    qk_local, value_local = weight_fold(
        query_key_weight, value_weight, row_products(normed), (qk_start, value_start)
    )
    qk_head = qk_local.reshape(tokens, 4, HD)
    value_head = value_local.astype(jnp.bfloat16)
    allowed = request_mask(lengths[0], tokens)
    head_out = diff_head(qk_head, value_head, allowed, head_second_weight[0])
    chosen = token_adapter_index[:, 0]
    owner_ids = jnp.arange(owners, dtype=jnp.int32)
    member = (chosen[:, None] == owner_ids[None, :]).astype(jnp.int32)
    earlier = jnp.cumsum(member, axis=0) - member
    within = jnp.sum(earlier * member, axis=1)
    target = chosen * capacity + within
    slot_ids = jnp.arange(owners * capacity, dtype=jnp.int32)
    dispatch = (slot_ids[:, None] == target[None, :]).astype(jnp.bfloat16)
    outgoing = jnp.dot(dispatch, head_out, preferred_element_type=jnp.float32).astype(jnp.bfloat16)
    outgoing = outgoing.reshape(owners, capacity, head_out.shape[1])
    received = lax.all_to_all(outgoing, "blk", split_axis=0, concat_axis=0, tiled=True)
    sources = received.shape[0]
    slot_count = received.shape[1]
    flat_heads_output = received.reshape(sources * slot_count, received.shape[2])
    reduced_rank_part = jnp.dot(
        flat_heads_output, adapter_down_maps[0], preferred_element_type=jnp.float32
    )
    reduced_rank_state = lax.psum(reduced_rank_part, "head").astype(jnp.bfloat16)
    adapter_delta = (
        adapter_scaling
        * jnp.dot(reduced_rank_state, adapter_up_maps[0], preferred_element_type=jnp.float32)
    ).astype(jnp.bfloat16)
    returned = lax.all_to_all(
        adapter_delta.reshape(sources, slot_count, width),
        "blk",
        split_axis=0,
        concat_axis=0,
        tiled=True,
    )
    delta_rows = lax.dot_general(
        dispatch,
        returned.reshape(owners * capacity, returned.shape[2]),
        (((0,), (0,)), ((), ())),
        preferred_element_type=jnp.float32,
    )
    delta_own = lax.dynamic_slice_in_dim(delta_rows, own_begin, own_width, 1)
    unit_count = down_weight.shape[1]

    def place_columns(totals, pieces, offset):
        columns = lax.dot_general(
            head_out, pieces[0], (((1,), (1,)), ((), ())), preferred_element_type=jnp.float32
        )
        return (columns, pieces[1])

    projected_start = jnp.zeros((tokens, width), jnp.float32)
    down_start = jnp.zeros((width, unit_count), jnp.bfloat16)
    projected, down_full = weight_fold(
        output_weight, down_weight, place_columns, (projected_start, down_start)
    )
    own_mid = (
        lax.dynamic_slice_in_dim(inputs, own_begin, own_width, 1)
        + head_total(projected)
        + delta_own
    )
    mid_full = lax.all_gather(own_mid.astype(jnp.bfloat16), "head", axis=1, tiled=True)
    ffn_in = (rms_scale(mid_full.astype(jnp.float32), 1e-06) * feedforward_norm_gain).astype(
        jnp.bfloat16
    )
    gate_start = jnp.zeros((tokens, gate_weight.shape[1]), jnp.float32)
    up_start = jnp.zeros((tokens, up_weight.shape[1]), jnp.float32)
    gate_act, upward = weight_fold(
        gate_weight, up_weight, row_products(ffn_in), (gate_start, up_start)
    )
    hidden_units = (jax.nn.silu(gate_act) * upward).astype(jnp.bfloat16)
    ffn_part = lax.dot_general(
        hidden_units, down_full, (((1,), (1,)), ((), ())), preferred_element_type=jnp.float32
    )
    return (own_mid + head_total(ffn_part)).astype(jnp.bfloat16)


def solution(mesh):
    return jax.shard_map(
        per_device,
        mesh=mesh,
        in_specs=(
            P("blk", None),
            P("blk", None),
            P("blk", None),
            P(),
            P("blk", "head"),
            P("blk", "head"),
            P("head"),
            P("blk", "head"),
            P("blk", "head", None),
            P("blk", None, None),
            P(),
            P("blk", "head"),
            P("blk", "head"),
            P("blk", "head"),
        ),
        out_specs=P("blk", "head"),
        check_vma=False,
    )
```

profile of v0, /device:TPU:2, one launch (start us, length us, event | category | flops | bytes accessed | tf_op | source)
XLA Modules:
  0.0 619.7 jit_solution(7784527970061427897)
XLA Ops:
  6.5 0.0 copy-start
  6.5 0.0 all-gather.7.cloned.1.call-start
  6.5 0.7 all-gather.7.cloned.1.call-update
  7.3 0.0 all-gather.9.cloned.1.call-start
  7.3 0.7 all-gather.9.cloned.1.call-update
  8.0 0.0 all-gather.11.cloned.1.call-start
  8.1 0.7 all-gather.11.cloned.1.call-update
  8.7 0.0 reduce-scatter.3.cloned.1.call-start
  8.8 0.8 reduce-window.18
  9.6 0.1 convert_reduce_fusion
  10.4 1.4 multiply_reduce_fusion
  11.7 86.2 %all-gather.7.cloned.1.call-done = bf16[2048,512]{1,0:T(8,128)(2,1)} async-done(((bf16[32,512]{1,0:T(8,128)(2,1)}), bf16[2048,512]{1,0:T(8,128)(2,1)}) %all-gather.7.cloned.1.call-update) | async-done | bytes 2097168 | tf_op jit(solution)/shard_map/all_gather | solution.py:50
  97.9 2.5 fusion.14
  100.4 0.0 copy-start.1
  100.4 0.0 copy-start.5
  100.4 0.1 reshape.92
  100.6 0.3 fusion.40
  100.8 0.4 fusion.42
  101.2 0.4 fusion.41
  101.6 0.1 fusion.22
  101.7 79.3 %all-gather.9.cloned.1.call-done = bf16[2048,256]{1,0:T(8,128)(2,1)} async-done(((bf16[32,256]{1,0:T(8,128)(2,1)}), bf16[2048,256]{1,0:T(8,128)(2,1)}) %all-gather.9.cloned.1.call-update) | async-done | bytes 1048592 | tf_op jit(solution)/shard_map/all_gather | solution.py:51
  181.0 0.0 copy-done.5
  181.0 2.0 multiply_reduce_fusion.1
  182.9 0.0 copy-start.3
  183.0 81.1 %all-gather.11.cloned.1.call-done = bf16[2048,256]{1,0:T(8,128)(2,1)} async-done(((bf16[32,256]{1,0:T(8,128)(2,1)}), bf16[2048,256]{1,0:T(8,128)(2,1)}) %all-gather.11.cloned.1.call-update) | async-done | bytes 1048592 | tf_op jit(solution)/shard_map/all_gather | solution.py:50
  264.1 2.7 convolution_convert_fusion.1
  266.8 0.0 reduce-scatter.3.cloned.1.call-update
  266.8 0.0 all-gather.13.cloned.1.call-start
  266.9 0.5 all-gather.13.cloned.1.call-update
  267.4 0.0 all-gather.15.cloned.1.call-start
  267.4 0.5 all-gather.15.cloned.1.call-update
  268.0 0.0 all-gather.17.cloned.1.call-start
  268.0 0.7 all-gather.17.cloned.1.call-update
  268.8 0.6 reduce-window.19
  269.4 0.2 slice_reduce_fusion
  269.6 0.1 bitcast_bitcast_fusion
  269.8 0.3 convolution_convert_fusion.2
  270.0 0.1 reshape.95
  270.1 19.7 %all_to_all.10 = bf16[64,6,256]{2,1,0:T(8,128)(2,1)S(1)} all-to-all(bf16[64,6,256]{2,1,0:T(8,128)(2,1)S(1)} %reshape.95), channel_id=1, replica_groups=mesh['head'=8,'blk'=64] {'blk'}, dimensions={0} | all-to-all | bytes 393216 | tf_op jit(solution)/shard_map/all_to_all | solution.py:117
  289.8 0.1 reshape.96
  289.9 0.2 fusion.35
  290.1 29.8 %psum.7 = bf16[384,16]{0,1:T(8,128)(2,1)S(1)} all-reduce(f32[384,16]{0,1:T(8,128)S(1)} %fusion.35), channel_id=1, replica_groups=mesh['head'=8,'blk'=64] {'head'}, use_global_device_ids=true, to_apply=%region_12.13 | all-reduce | flops 6144 | bytes 36864 | tf_op jit(solution)/shard_map/psum | solution.py:124
  319.8 0.0 copy-done
  319.9 0.6 multiply_convert_fusion
  320.4 1.6 reshape.97
  322.0 5.6 all-to-all-start.1
  327.7 0.0 reduce-scatter.5.cloned.1.call-start
  327.7 1.4 convert_element_type.59
  329.1 54.3 %all-to-all-done.1 = bf16[64,6,2048]{2,1,0:T(8,128)(2,1)S(1)} async-done(((bf16[64,6,2048]{2,1,0:T(8,128)(2,1)}), bf16[64,6,2048]{2,1,0:T(8,128)(2,1)S(1)}, u32[]{:S(2)}, u32[]{:S(2)}) %all-to-all-start.1) | async-done | bytes 1572896 | tf_op jit(solution)/shard_map/all_to_all | solution.py:129
  383.4 1.4 reshape.98
  384.8 2.0 fusion.12
  386.9 0.0 copy-start.6
  386.9 0.0 reduce-scatter.3.cloned.1.call-done
  386.9 1.0 fusion.37
  388.0 26.0 %all_gather.24 = bf16[192,2048]{1,0:T(8,128)(2,1)S(1)} all-gather(bf16[192,256]{1,0:T(8,128)(2,1)S(1)} %fusion.37), channel_id=1, replica_groups=mesh['head'=8,'blk'=64] {'head'}, dimensions={1}, use_global_device_ids=true | all-gather | bytes 884736 | tf_op jit(solution)/shard_map/all_gather | solution.py:161
  413.9 0.2 fusion
  414.2 0.0 all-gather.13.cloned.1.call-done
  414.2 2.7 fusion.17
  417.0 64.8 %all-gather.15.cloned.1.call-done = bf16[2048,704]{1,0:T(8,128)(2,1)} async-done(((bf16[32,704]{1,0:T(8,128)(2,1)}), bf16[2048,704]{1,0:T(8,128)(2,1)}) %all-gather.15.cloned.1.call-update) | async-done | bytes 2883600 | tf_op jit(solution)/shard_map/all_gather | solution.py:51
  481.7 85.3 %all-gather.17.cloned.1.call-done = bf16[2048,704]{1,0:T(8,128)(2,1)} async-done(((bf16[32,704]{1,0:T(8,128)(2,1)}), bf16[2048,704]{1,0:T(8,128)(2,1)}) %all-gather.17.cloned.1.call-update) | async-done | bytes 2883600 | tf_op jit(solution)/shard_map/all_gather | solution.py:51
  567.0 5.7 convolution_convert_fusion
  572.7 0.0 reduce-scatter.5.cloned.1.call-update
  572.8 38.4 %reduce-scatter.5.cloned.1.call-done = bf16[192,256]{1,0:T(8,128)(2,1)} async-done(((bf16[192,2048]{1,0:T(8,128)(2,1)}), bf16[192,256]{1,0:T(8,128)(2,1)}) %reduce-scatter.5.cloned.1.call-update) | async-done | bytes 98320 | tf_op jit(solution)/shard_map/reduce_scatter | solution.py:58
  611.2 1.7 add_convert_fusion
  (16 shorter events, 0.1 us)
Async XLA Ops:
  6.5 313.3 %copy-start = (bf16[1,16,2048]{2,1,0:T(8,128)(2,1)S(1)}, bf16[1,16,2048]{2,1,0:T(8,128)(2,1)}, u32[]{:S(2)}) copy-start(bf16[1,16,2048]{2,1,0:T(8,128)(2,1)} %param.23) | copy-start | bytes 196612
  6.5 91.4 %all-gather.7.cloned.1.call-start = ((), (), s32[]{:S(2)}) async-start(), calls=%async_computation.4 | async-start | bytes 2129920 | tf_op jit(solution)/shard_map/all_gather | solution.py:50
  7.3 173.7 %all-gather.9.cloned.1.call-start = ((), (), s32[]{:S(2)}) async-start(), calls=%async_computation.5 | async-start | bytes 1064960 | tf_op jit(solution)/shard_map/all_gather | solution.py:51
  8.0 256.1 %all-gather.11.cloned.1.call-start = ((), (), s32[]{:S(2)}) async-start(), calls=%async_computation.6 | async-start | bytes 1064960 | tf_op jit(solution)/shard_map/all_gather | solution.py:50
  8.7 378.2 %reduce-scatter.3.cloned.1.call-start = ((), (), s32[]{:S(2)}) async-start(), calls=%async_computation.7 | async-start | bytes 884736 | tf_op jit(solution)/shard_map/reduce_scatter | solution.py:58
  100.4 80.6 %copy-start.1 = (bf16[192,2048]{1,0:T(8,128)(2,1)S(1)}, bf16[192,2048]{1,0:T(8,128)(2,1)}, u32[]{:S(2)}) copy-start(bf16[192,2048]{1,0:T(8,128)(2,1)} %param.14) | copy-start | bytes 2359300
  100.4 80.6 %copy-start.5 = (f32[2048]{0:T(1024)S(1)}, f32[2048]{0:T(1024)}, u32[]{:S(2)}) copy-start(f32[2048]{0:T(1024)} %param.17) | copy-start | bytes 24580
  182.9 85.8 %copy-start.3 = (s32[192,1]{0,1:T(1,128)S(1)}, s32[192,1]{0,1:T(1,128)}, u32[]{:S(2)}) copy-start(s32[192,1]{0,1:T(1,128)} %param.16) | copy-start | bytes 2308
  266.8 23.1 %copy-start.4 = (bf16[1,256,16]{1,2,0:T(8,128)(2,1)S(1)}, bf16[1,256,16]{1,2,0:T(8,128)(2,1)}, u32[]{:S(2)}) copy-start(bf16[1,256,16]{1,2,0:T(8,128)(2,1)} %param.22) | copy-start | bytes 24580
  266.8 147.4 %all-gather.13.cloned.1.call-start = ((), (), s32[]{:S(2)}) async-start(), calls=%async_computation.8 | async-start | bytes 3194880 | tf_op jit(solution)/shard_map/all_gather | solution.py:50
  267.4 214.3 %all-gather.15.cloned.1.call-start = ((), (), s32[]{:S(2)}) async-start(), calls=%async_computation.9 | async-start | bytes 3194880 | tf_op jit(solution)/shard_map/all_gather | solution.py:51
  268.0 299.0 %all-gather.17.cloned.1.call-start = ((), (), s32[]{:S(2)}) async-start(), calls=%async_computation.10 | async-start | bytes 3194880 | tf_op jit(solution)/shard_map/all_gather | solution.py:51
  322.0 61.4 %all-to-all-start.1 = ((bf16[64,6,2048]{2,1,0:T(8,128)(2,1)}), bf16[64,6,2048]{2,1,0:T(8,128)(2,1)S(1)}, u32[]{:S(2)}, u32[]{:S(2)}) async-start(bf16[64,6,2048]{2,1,0:T(8,128)(2,1)} %reshape.97), calls=%async_computation.2 | async-start | bytes 4194304 | tf_op jit(solution)/shard_map/all_to_all | solution.py:129
  327.7 283.5 %reduce-scatter.5.cloned.1.call-start = ((), (), s32[]{:S(2)}) async-start(), calls=%async_computation.11 | async-start | bytes 884736 | tf_op jit(solution)/shard_map/reduce_scatter | solution.py:58
  386.9 27.3 %copy-start.6 = (f32[2048]{0:T(1024)S(1)}, f32[2048]{0:T(1024)}, u32[]{:S(2)}) copy-start(f32[2048]{0:T(1024)} %param.24) | copy-start | bytes 24580
  416.9 194.2 %copy-start.2 = (bf16[192,256]{1,0:T(8,128)(2,1)S(1)}, bf16[192,256]{1,0:T(8,128)(2,1)}, u32[]{:S(2)}) copy-start(bf16[192,256]{1,0:T(8,128)(2,1)} %reduce-scatter.3.cloned.1.call-done) | copy-start | bytes 294916
Sparse Core Ops, SparseCore 0:
  10.7 87.1 all-gather.6
  101.3 79.6 all-gather.8
  184.3 79.7 all-gather.10
  266.9 38.3 reduce-scatter.2
  309.0 88.1 all-gather.12
  400.9 80.8 all-gather.14
  485.6 81.3 all-gather.16
  572.9 38.2 reduce-scatter.4
where the time goes:
time: 620 us
  waiting for transfers between devices  493 us (80%)
  blocking collectives  75.5 us (12%)
  matrix products  19.4 us (3%)
  between operations  14.3 us (2%)
  other arithmetic  7.53 us (1%)
    all_gather x3, waiting for transfers between devices, weight_fold(): lax.all_gather(trailing, 'blk', axis=0, tiled=True)  229 us
    all_gather x3, waiting for transfers between devices, weight_fold(): lax.all_gather(leading, 'blk', axis=0, tiled=True)  167 us
    all_to_all x1, waiting for transfers between devices, per_device(): lax.all_to_all(adapter_delta.reshape(sources, slot_count, width), 'blk',...  54.3 us
    reduce_scatter x2, waiting for transfers between devices, head_total(): lax.psum_scatter(partial_value.astype(jnp.bfloat16), 'head', scatter_dime...  38.4 us
    psum x1, blocking collectives, per_device(): lax.psum(reduced_rank_part, 'head').astype(jnp.bfloat16)  29.8 us
    all_gather x1, blocking collectives, per_device(): lax.all_gather(own_mid.astype(jnp.bfloat16), 'head', axis=1, tiled=True)  26 us
    all_to_all x1, blocking collectives, per_device(): lax.all_to_all(outgoing, 'blk', split_axis=0, concat_axis=0, tiled=True)  19.7 us
  transfers between devices with their start and end apart: 9, of which 7 were waited for; matrix products, arithmetic and copies ran while one was open for 3% of the time, Pallas kernels for 0%

commit v1 on v0

--- a/solution.py
+++ b/solution.py
@@ -48,7 +48,9 @@
         initial,
         (
             lax.all_gather(leading, "blk", axis=0, tiled=True),
-            lax.all_gather(trailing, "blk", axis=0, tiled=True),
+            jnp.concatenate(
+                lax.all_to_all(jnp.stack([trailing] * lax.axis_size("blk")), "blk", 0, 0), axis=0
+            ),
         ),
         jnp.int32(0),
     )

time: 620 us -> 418 us (0.67)
  waiting for transfers between devices: 493 us -> 261 us
  starting transfers between devices: 5.91 us -> 31.8 us
    all_gather x3 -> x0, waiting for transfers between devices: 229 us -> none  [weight_fold(): lax.all_gather(trailing, 'blk', axis=0, tiled=True)]
    all_to_all x0 -> x3, waiting for transfers between devices: none -> 42.2 us  [weight_fold(): lax.all_to_all(jnp.stack([trailing] * lax.axis_size('blk')), 'blk', 0, 0)]
    all_to_all x0 -> x3, starting transfers between devices: none -> 26.3 us  [weight_fold(): lax.all_to_all(jnp.stack([trailing] * lax.axis_size('blk')), 'blk', 0, 0)]
    all_gather x3, waiting for transfers between devices: 167 us -> 141 us  [weight_fold(): lax.all_gather(leading, 'blk', axis=0, tiled=True)]
    all_to_all x1, waiting for transfers between devices: 54.3 us -> 36.5 us  [per_device(): lax.all_to_all(adapter_delta.reshape(sources, slot_count, width), 'blk',...]
  transfers between devices with their start and end apart: 9 -> 9, of which waited for: 7 -> 6; matrix products, arithmetic and copies ran while one was open for 3% -> 5% of each run, Pallas kernels for 0% -> 0%
where the time goes in v1:
time: 418 us; the launch traced here: 417 us
  waiting for transfers between devices  261 us (62%)
  blocking collectives  76.7 us (18%)
  starting transfers between devices  31.8 us (8%)
  matrix products  17.9 us (4%)
  between operations  14.1 us (3%)
  local copies, waits for them, and re-layouts  9.81 us (2%)
  other arithmetic  5.75 us (1%)
    all_gather x3, waiting for transfers between devices, weight_fold(): lax.all_gather(leading, 'blk', axis=0, tiled=True)  141 us
    all_to_all x3, waiting for transfers between devices, weight_fold(): lax.all_to_all(jnp.stack([trailing] * lax.axis_size('blk')), 'blk', 0, 0)  42.2 us
    reduce_scatter x2, waiting for transfers between devices, head_total(): lax.psum_scatter(partial_value.astype(jnp.bfloat16), 'head', scatter_dime...  39.2 us
    all_to_all x1, waiting for transfers between devices, per_device(): lax.all_to_all(adapter_delta.reshape(sources, slot_count, width), 'blk',...  36.5 us
    psum x1, blocking collectives, per_device(): lax.psum(reduced_rank_part, 'head').astype(jnp.bfloat16)  29.8 us
    all_gather x1, blocking collectives, per_device(): lax.all_gather(own_mid.astype(jnp.bfloat16), 'head', axis=1, tiled=True)  27.2 us
    all_to_all x3, starting transfers between devices, weight_fold(): lax.all_to_all(jnp.stack([trailing] * lax.axis_size('blk')), 'blk', 0, 0)  26.3 us
    all_to_all x1, blocking collectives, per_device(): lax.all_to_all(outgoing, 'blk', split_axis=0, concat_axis=0, tiled=True)  19.7 us
  transfers between devices with their start and end apart: 9, of which 6 were waited for; matrix products, arithmetic and copies ran while one was open for 5% of the time, Pallas kernels for 0%

profile of v1, /device:TPU:2, one launch (start us, length us, event | category | flops | bytes accessed | tf_op | source)
XLA Modules:
  0.0 417.1 jit_solution(14730130877273883059)
XLA Ops:
  6.5 0.0 copy-start
  6.5 0.0 all-gather.4.cloned.1.call-start
  6.5 0.7 all-gather.4.cloned.1.call-update
  7.3 0.0 copy-start.5
  7.3 1.9 stack.6
  9.2 14.0 %all-to-all-start = ((bf16[64,32,256]{2,1,0:T(8,128)(2,1)}), bf16[64,32,256]{2,1,0:T(8,128)(2,1)S(1)}, u32[]{:S(2)}, u32[]{:S(2)}) async-start(bf16[64,32,256]{2,1,0:T(8,128)(2,1)} %stack.6), calls=%async_computation | async-start | bytes 2097152 | tf_op jit(solution)/shard_map/all_to_all | solution.py:52
  23.2 0.6 reduce-window.19
  23.9 0.2 slice_reduce_fusion
  24.1 0.2 reduce-window.18
  24.9 0.1 convert_reduce_fusion
  25.0 0.1 bitcast_bitcast_fusion
  25.1 0.0 copy-done.1
  25.1 0.2 multiply_reduce_fusion
  25.4 73.9 %all-gather.4.cloned.1.call-done = bf16[2048,512]{1,0:T(8,128)(2,1)} async-done(((bf16[32,512]{1,0:T(8,128)(2,1)}), bf16[2048,512]{1,0:T(8,128)(2,1)}) %all-gather.4.cloned.1.call-update) | async-done | bytes 2097168 | tf_op jit(solution)/shard_map/all_gather | solution.py:50
  99.3 2.2 fusion.14
  101.5 0.1 reshape.107
  101.7 0.3 fusion.40
  102.0 0.4 fusion.41
  102.3 0.4 fusion.42
  102.7 0.1 fusion.22
  102.9 0.0 all-to-all-done
  102.9 0.0 copy-start.3
  102.9 0.7 multiply_reduce_fusion.1
  103.6 0.3 convolution_convert_fusion.2
  103.9 0.1 reshape.111
  104.0 19.7 %all_to_all.25 = bf16[64,6,256]{2,1,0:T(8,128)(2,1)S(1)} all-to-all(bf16[64,6,256]{2,1,0:T(8,128)(2,1)S(1)} %reshape.111), channel_id=1, replica_groups=mesh['head'=8,'blk'=64] {'blk'}, dimensions={0} | all-to-all | bytes 393216 | tf_op jit(solution)/shard_map/all_to_all | solution.py:119
  123.7 2.1 stack.8
  125.8 6.3 %all-to-all-start.4 = ((bf16[64,32,704]{2,1,0:T(8,128)(2,1)}), bf16[64,32,704]{2,1,0:T(8,128)(2,1)}, u32[]{:S(2)}, u32[]{:S(2)}) async-start(bf16[64,32,704]{2,1,0:T(8,128)(2,1)} %stack.8), calls=%async_computation.5 | async-start | bytes 6291456 | tf_op jit(solution)/shard_map/all_to_all | solution.py:52
  132.1 0.0 all-gather.6.cloned.1.call-start
  132.1 0.7 all-gather.6.cloned.1.call-update
  132.8 0.1 reshape.112
  132.9 0.2 fusion.35
  133.0 29.8 %psum.7 = bf16[384,16]{0,1:T(8,128)(2,1)S(1)} all-reduce(f32[384,16]{0,1:T(8,128)S(1)} %fusion.35), channel_id=1, replica_groups=mesh['head'=8,'blk'=64] {'head'}, use_global_device_ids=true, to_apply=%region_12.13 | all-reduce | flops 6144 | bytes 36864 | tf_op jit(solution)/shard_map/psum | solution.py:126
  162.8 0.6 multiply_convert_fusion
  163.4 1.6 reshape.113
  165.0 42.2 %all-to-all-done.4 = bf16[64,32,704]{2,1,0:T(8,128)(2,1)} async-done(((bf16[64,32,704]{2,1,0:T(8,128)(2,1)}), bf16[64,32,704]{2,1,0:T(8,128)(2,1)}, u32[]{:S(2)}, u32[]{:S(2)}) %all-to-all-start.4) | async-done | bytes 2883616 | tf_op jit(solution)/shard_map/all_to_all | solution.py:52
  207.2 5.4 %all-to-all-start.2 = ((bf16[64,6,2048]{2,1,0:T(8,128)(2,1)}), bf16[64,6,2048]{2,1,0:T(8,128)(2,1)S(1)}, u32[]{:S(2)}, u32[]{:S(2)}) async-start(bf16[64,6,2048]{2,1,0:T(8,128)(2,1)} %reshape.113), calls=%async_computation.3 | async-start | bytes 4194304 | tf_op jit(solution)/shard_map/all_to_all | solution.py:131
  212.6 0.0 copy-start.4
  212.6 0.0 reduce-scatter.3.cloned.1.call-start
  212.7 11.4 %all-gather.6.cloned.1.call-done = bf16[2048,256]{1,0:T(8,128)(2,1)} async-done(((bf16[32,256]{1,0:T(8,128)(2,1)}), bf16[2048,256]{1,0:T(8,128)(2,1)}) %all-gather.6.cloned.1.call-update) | async-done | bytes 1048592 | tf_op jit(solution)/shard_map/all_gather | solution.py:50
  224.1 2.6 convolution_convert_fusion.1
  226.7 0.0 reduce-scatter.3.cloned.1.call-update
  226.7 0.0 all-gather.8.cloned.1.call-start
  226.8 0.5 all-gather.8.cloned.1.call-update
  227.3 36.5 %all-to-all-done.2 = bf16[64,6,2048]{2,1,0:T(8,128)(2,1)S(1)} async-done(((bf16[64,6,2048]{2,1,0:T(8,128)(2,1)}), bf16[64,6,2048]{2,1,0:T(8,128)(2,1)S(1)}, u32[]{:S(2)}, u32[]{:S(2)}) %all-to-all-start.2) | async-done | bytes 1572896 | tf_op jit(solution)/shard_map/all_to_all | solution.py:131
  263.8 0.0 copy-done.4
  263.8 2.0 stack.7
  265.8 6.0 %all-to-all-start.3 = ((bf16[64,32,704]{2,1,0:T(8,128)(2,1)}), bf16[64,32,704]{2,1,0:T(8,128)(2,1)}, u32[]{:S(2)}, u32[]{:S(2)}) async-start(bf16[64,32,704]{2,1,0:T(8,128)(2,1)} %stack.7), calls=%async_computation.4 | async-start | bytes 6291456 | tf_op jit(solution)/shard_map/all_to_all | solution.py:52
  271.8 0.0 reduce-scatter.5.cloned.1.call-start
  271.9 1.4 convert_element_type.59
  273.2 1.4 reshape.114
  274.7 2.0 fusion.12
  276.7 0.0 copy-start.8
  276.7 0.0 reduce-scatter.3.cloned.1.call-done
  276.7 1.0 fusion.37
  277.7 27.2 %all_gather.14 = bf16[192,2048]{1,0:T(8,128)(2,1)S(1)} all-gather(bf16[192,256]{1,0:T(8,128)(2,1)S(1)} %fusion.37), channel_id=1, replica_groups=mesh['head'=8,'blk'=64] {'head'}, dimensions={1}, use_global_device_ids=true | all-gather | bytes 884736 | tf_op jit(solution)/shard_map/all_gather | solution.py:163
  305.0 0.2 fusion
  305.2 56.0 %all-gather.8.cloned.1.call-done = bf16[2048,704]{1,0:T(8,128)(2,1)} async-done(((bf16[32,704]{1,0:T(8,128)(2,1)}), bf16[2048,704]{1,0:T(8,128)(2,1)}) %all-gather.8.cloned.1.call-update) | async-done | bytes 2883600 | tf_op jit(solution)/shard_map/all_gather | solution.py:50
  361.2 2.7 fusion.17
  363.9 0.0 all-to-all-done.3
  363.9 5.8 %convolution_convert_fusion = bf16[192,2048]{1,0:T(8,128)(2,1)} fusion(bf16[2048,704]{1,0:T(8,128)(2,1)} %bitcast.13, bf16[2048,704]{1,0:T(8,128)(2,1)} %bitcast.12, f32[192,704]{1,0:T(8,128)S(1)} %fusion.17, bf16[192,2048]{1,0:T(8,128)(2,1)S(1)} %all_gather.14, f32[2048]{0:T(1024)S(1)} %copy-done.8, f32[192]{0:T(256)S(1)} %add_rsqrt_fusion), kind=kOutput, calls=%fused_computation.1 | convolution fusion | flops 1110073344 | bytes 7889664 | tf_op jit(solution)/shard_map/dot_general | solution.py:173
  369.7 0.0 reduce-scatter.5.cloned.1.call-update
  369.8 39.2 %reduce-scatter.5.cloned.1.call-done = bf16[192,256]{1,0:T(8,128)(2,1)} async-done(((bf16[192,2048]{1,0:T(8,128)(2,1)}), bf16[192,256]{1,0:T(8,128)(2,1)}) %reduce-scatter.5.cloned.1.call-update) | async-done | bytes 98320 | tf_op jit(solution)/shard_map/reduce_scatter | solution.py:60
  408.9 1.7 add_convert_fusion
  (22 shorter events, 0.2 us)
Async XLA Ops:
  6.5 156.3 %copy-start = (bf16[1,16,2048]{2,1,0:T(8,128)(2,1)S(1)}, bf16[1,16,2048]{2,1,0:T(8,128)(2,1)}, u32[]{:S(2)}) copy-start(bf16[1,16,2048]{2,1,0:T(8,128)(2,1)} %param.23) | copy-start | bytes 196612
  6.5 92.8 %all-gather.4.cloned.1.call-start = ((), (), s32[]{:S(2)}) async-start(), calls=%async_computation.7 | async-start | bytes 2129920 | tf_op jit(solution)/shard_map/all_gather | solution.py:50
  7.3 15.9 %copy-start.5 = (s32[192,1]{0,1:T(1,128)S(1)}, s32[192,1]{0,1:T(1,128)}, u32[]{:S(2)}) copy-start(s32[192,1]{0,1:T(1,128)} %param.16) | copy-start | bytes 2308
  7.3 16.8 %copy-start.9 = (s32[1,6]{1,0:T(1,128)S(1)}, s32[1,6]{1,0:T(1,128)}, u32[]{:S(2)}) copy-start(s32[1,6]{1,0:T(1,128)} %param.15) | copy-start | bytes 76
  7.3 17.9 %copy-start.1 = (bf16[192,2048]{1,0:T(8,128)(2,1)S(1)}, bf16[192,2048]{1,0:T(8,128)(2,1)}, u32[]{:S(2)}) copy-start(bf16[192,2048]{1,0:T(8,128)(2,1)} %param.14) | copy-start | bytes 2359300
  9.2 90.1 %copy-start.7 = (f32[2048]{0:T(1024)S(1)}, f32[2048]{0:T(1024)}, u32[]{:S(2)}) copy-start(f32[2048]{0:T(1024)} %param.17) | copy-start | bytes 24580
  9.2 93.7 %all-to-all-start = ((bf16[64,32,256]{2,1,0:T(8,128)(2,1)}), bf16[64,32,256]{2,1,0:T(8,128)(2,1)S(1)}, u32[]{:S(2)}, u32[]{:S(2)}) async-start(bf16[64,32,256]{2,1,0:T(8,128)(2,1)} %stack.6), calls=%async_computation | async-start | bytes 2097152 | tf_op jit(solution)/shard_map/all_to_all | solution.py:52
  102.9 20.8 %copy-start.3 = (bf16[32,704]{1,0:T(8,128)(2,1)S(1)}, bf16[32,704]{1,0:T(8,128)(2,1)}, u32[]{:S(2)}) copy-start(bf16[32,704]{1,0:T(8,128)(2,1)} %param.27) | copy-start | bytes 135172
  125.8 7.1 %copy-start.6 = (bf16[1,256,16]{1,2,0:T(8,128)(2,1)S(1)}, bf16[1,256,16]{1,2,0:T(8,128)(2,1)}, u32[]{:S(2)}) copy-start(bf16[1,256,16]{1,2,0:T(8,128)(2,1)} %param.22) | copy-start | bytes 24580
  125.8 81.5 %all-to-all-start.4 = ((bf16[64,32,704]{2,1,0:T(8,128)(2,1)}), bf16[64,32,704]{2,1,0:T(8,128)(2,1)}, u32[]{:S(2)}, u32[]{:S(2)}) async-start(bf16[64,32,704]{2,1,0:T(8,128)(2,1)} %stack.8), calls=%async_computation.5 | async-start | bytes 6291456 | tf_op jit(solution)/shard_map/all_to_all | solution.py:52
  132.1 92.0 %all-gather.6.cloned.1.call-start = ((), (), s32[]{:S(2)}) async-start(), calls=%async_computation.8 | async-start | bytes 1064960 | tf_op jit(solution)/shard_map/all_gather | solution.py:50
  207.2 56.6 %all-to-all-start.2 = ((bf16[64,6,2048]{2,1,0:T(8,128)(2,1)}), bf16[64,6,2048]{2,1,0:T(8,128)(2,1)S(1)}, u32[]{:S(2)}, u32[]{:S(2)}) async-start(bf16[64,6,2048]{2,1,0:T(8,128)(2,1)} %reshape.113), calls=%async_computation.3 | async-start | bytes 4194304 | tf_op jit(solution)/shard_map/all_to_all | solution.py:131
  212.6 51.2 %copy-start.4 = (bf16[32,704]{1,0:T(8,128)(2,1)S(1)}, bf16[32,704]{1,0:T(8,128)(2,1)}, u32[]{:S(2)}) copy-start(bf16[32,704]{1,0:T(8,128)(2,1)} %param.26) | copy-start | bytes 135172
  212.6 64.1 %reduce-scatter.3.cloned.1.call-start = ((), (), s32[]{:S(2)}) async-start(), calls=%async_computation.9 | async-start | bytes 884736 | tf_op jit(solution)/shard_map/reduce_scatter | solution.py:60
  226.7 134.5 %all-gather.8.cloned.1.call-start = ((), (), s32[]{:S(2)}) async-start(), calls=%async_computation.10 | async-start | bytes 3194880 | tf_op jit(solution)/shard_map/all_gather | solution.py:50
  265.8 98.1 %all-to-all-start.3 = ((bf16[64,32,704]{2,1,0:T(8,128)(2,1)}), bf16[64,32,704]{2,1,0:T(8,128)(2,1)}, u32[]{:S(2)}, u32[]{:S(2)}) async-start(bf16[64,32,704]{2,1,0:T(8,128)(2,1)} %stack.7), calls=%async_computation.4 | async-start | bytes 6291456 | tf_op jit(solution)/shard_map/all_to_all | solution.py:52
  271.8 137.1 %reduce-scatter.5.cloned.1.call-start = ((), (), s32[]{:S(2)}) async-start(), calls=%async_computation.11 | async-start | bytes 884736 | tf_op jit(solution)/shard_map/reduce_scatter | solution.py:60
  276.7 84.5 %copy-start.8 = (f32[2048]{0:T(1024)S(1)}, f32[2048]{0:T(1024)}, u32[]{:S(2)}) copy-start(f32[2048]{0:T(1024)} %param.24) | copy-start | bytes 24580
  363.9 45.0 %copy-start.2 = (bf16[192,256]{1,0:T(8,128)(2,1)S(1)}, bf16[192,256]{1,0:T(8,128)(2,1)}, u32[]{:S(2)}) copy-start(bf16[192,256]{1,0:T(8,128)(2,1)} %reduce-scatter.3.cloned.1.call-done) | copy-start | bytes 294916
Sparse Core Ops, SparseCore 0:
  10.7 88.5 all-gather.3
  136.3 87.7 all-gather.5
  226.9 38.9 reduce-scatter.2
  269.7 91.4 all-gather.7
  369.9 39.0 reduce-scatter.4
